TPU v7x, 256 devices: a whole 4x4x8 slice. The times are simulated.
256 devices in a mesh: grp: 4 (over z_hi), gx: 32 (over x, z_lo, y), gy: 2 (over core).
Axes of the slice: x: 4, y: 4, z: 8 (z_hi: 4, z_lo: 2; z = z_hi * 2 + z_lo), core: 2. Of those that a mesh axis runs over, the one named last changes fastest.
Arguments:
- fluid_temp: float32 [512, 256, 1024], P('gx', 'gy', 'grp'), may hold values from -6 to 6
- active: int32 [512, 256, 1024], P('gx', 'gy', 'grp'), may hold values 0 or 1
- fin_temp: float32 [256, 1024, 512], P('grp', 'gx', 'gy'), may hold values from -6 to 6
- fin_source: float32 [256, 1024, 512], P('grp', 'gx', 'gy'), may hold values from -6 to 6
- wall_owner: int32 [32, 2, 2048, 1], P('gx', 'gy'), may hold values from 0 to 31, as said below
- wall_target: int32 [32, 2, 2048], P('gx', 'gy'), may hold values from 0 to 8191, as said below
Outputs:
- fluid_new: float32 [512, 256, 1024], P('gx', 'gy', 'grp')
- fin_new: float32 [256, 1024, 512], P('grp', 'gx', 'gy')
Inputs may be any that keep to these rules, and one draw needn't show every extreme that they name: `wall_owner`: among the 2048 wall cells of one column block (a, b), exactly 128 name the owner a and at most 128 name any one owner; in every draw one owner is named by exactly 128 wall cells of every column block. `wall_target`: wall cell w = i * 128 + j names a root cell (2 * i + di) * 256 + 2 * j + dj of the 2 x 2 patch beneath it, di and dj being 0 or 1; the first wall cell of a block names its patch's first root cell, the last one its patch's last.
All inputs are finite; a program needn't handle non-finite values. No bound on the sum of `active` on one device may be relied on, other than what follows from the above.
Results may differ from a plain program's by a relative error of at most 0.00002.
Values sent between devices are 32-bit elements; how exact they have to be, the bound alone decides.
A program may use at most 64 MiB of HBM per device.

v0:
```python
import jax
import jax.numpy as jnp
from jax import lax
from jax.sharding import PartitionSpec as P

FLUID_DIFFUSION = 1.0
FIN_CONDUCTION = 1.0
HEAT_COEF = 1.0


def padded_2(block, sides, width):
    for axis, dim in sides:
        count = lax.axis_size(axis)
        forward = [(i, i + 1) for i in range(count - 1)]
        backward = [(target, source) for source, target in forward]
        low = lax.ppermute(
            lax.slice_in_dim(block, block.shape[dim] - width, None, axis=dim), axis, forward
        )
        high = lax.ppermute(lax.slice_in_dim(block, 0, width, axis=dim), axis, backward)
        block = jnp.concatenate([low, block, high], axis=dim)
    return block


def six_sum(padded):
    return (
        padded[2:, 1:-1, 1:-1]
        + padded[:-2, 1:-1, 1:-1]
        + padded[1:-1, 2:, 1:-1]
        + padded[1:-1, :-2, 1:-1]
        + padded[1:-1, 1:-1, 2:]
        + padded[1:-1, 1:-1, :-2]
    )


def fin_from_padded(padded, field):
    return (1.0 + 6.0 * FIN_CONDUCTION) * field - FIN_CONDUCTION * six_sum(padded)


def fin_image(field):
    padded = padded_2(field, (("grp", 0), ("gx", 1), ("gy", 2)), 1)
    return fin_from_padded(padded, field)


def fluid_padded_apart(field):
    return padded_2(field, (("grp", 2), ("gx", 0), ("gy", 1)), 1)


def fluid_update(padded, field, fluid_temp, update_mask, ghost, on_wall):
    lowest = lax.broadcasted_iota(jnp.int32, field.shape, 2) == 0
    below = jnp.where(lowest & on_wall, ghost[:, :, None], 0.0)
    neighbours = six_sum(padded) + below
    updated = (fluid_temp + FLUID_DIFFUSION * neighbours) / (1.0 + 6.0 * FLUID_DIFFUSION)
    return jnp.where(update_mask, updated, field)


def local(fluid_temp, active, fin_temp, fin_source, wall_owner, wall_target):
    first_cells, second_cells, third_cells = fluid_temp.shape
    fin_depth, fin_width, fin_height = fin_temp.shape
    owner_count = lax.axis_size("gx")
    wall_cells = first_cells * second_cells
    capacity = min(wall_cells, max(2, 2 * wall_cells // owner_count))
    on_wall = lax.axis_index("grp") == 0
    owners = wall_owner[0, 0, :, 0]
    targets = wall_target[0, 0, :]
    onehot = (owners[:, None] == jnp.arange(owner_count, dtype=jnp.int32)[None, :]).astype(
        jnp.int32
    )
    ranks = jnp.sum((jnp.cumsum(onehot, axis=0) - onehot) * onehot, axis=1)
    slot_index = owners * capacity + ranks
    wall_temps = fluid_temp[:, :, 0].reshape(-1)
    send_temps = jnp.zeros((owner_count * capacity,), jnp.float32).at[slot_index].set(wall_temps)
    send_targets = (
        jnp.full((owner_count * capacity,), -1.0, jnp.float32)
        .at[slot_index]
        .set(targets.astype(jnp.float32))
    )
    received = lax.all_to_all(
        jnp.stack([send_temps, send_targets]), "gx", split_axis=1, concat_axis=1, tiled=True
    )
    got_targets = received[1].astype(jnp.int32)
    valid = (got_targets >= 0) & on_wall
    safe_targets = jnp.where(valid, got_targets, 0)
    surface = fin_temp[0].reshape(-1)
    fin_wall = jnp.where(valid, surface[safe_targets], 0.0)
    heat_flux = jnp.where(valid, HEAT_COEF * (received[0] - fin_wall), 0.0)
    deposit = jax.ops.segment_sum(heat_flux, safe_targets, num_segments=fin_width * fin_height)
    returned = lax.all_to_all(fin_wall, "gx", split_axis=0, concat_axis=0, tiled=True)
    ghost = returned[slot_index].reshape(first_cells, second_cells)
    fin_rhs = fin_temp + fin_source
    fin_rhs = fin_rhs.at[0].add(deposit.reshape(fin_width, fin_height))
    diag = 1.0 + 6.0 * FIN_CONDUCTION
    spectral = 6.0 * FIN_CONDUCTION / diag
    omega = 1.0 / (1.0 - spectral * spectral / 2.0)
    shape = fluid_temp.shape
    colour = (
        lax.broadcasted_iota(jnp.int32, shape, 0)
        + lax.broadcasted_iota(jnp.int32, shape, 1)
        + lax.broadcasted_iota(jnp.int32, shape, 2)
    ) % 2
    red_mask = (colour == 0) & (active == 1)
    black_mask = (colour == 1) & (active == 1)
    first_state = fin_temp + (fin_rhs - fin_image(fin_temp)) / diag
    second_image = fin_image(first_state)
    red_temp = fluid_update(
        fluid_padded_apart(fluid_temp), fluid_temp, fluid_temp, red_mask, ghost, on_wall
    )
    fluid_new = fluid_update(
        fluid_padded_apart(red_temp), red_temp, fluid_temp, black_mask, ghost, on_wall
    )
    fin_new = omega * (first_state + (fin_rhs - second_image) / diag - fin_temp) + fin_temp
    return (fluid_new, fin_new)


def solution(mesh):
    in_specs = (
        P("gx", "gy", "grp"),
        P("gx", "gy", "grp"),
        P("grp", "gx", "gy"),
        P("grp", "gx", "gy"),
        P("gx", "gy", None, None),
        P("gx", "gy", None),
    )
    out_specs = (P("gx", "gy", "grp"), P("grp", "gx", "gy"))
    return jax.shard_map(local, mesh=mesh, in_specs=in_specs, out_specs=out_specs, check_vma=False)
```

profile of v0, /device:TPU:120, one launch (start us, length us, event | category | flops | bytes accessed | tf_op | source)
XLA Modules:
  0.0 321.8 jit_solution(9975414038074076085)
XLA Ops:
  0.6 1.9 fusion.54
  2.9 1.9 collective-permute-start.1
  4.9 9.1 %reduce-window.6 = s32[32,16,128]{2,1,0:T(8,128)S(1)} reduce-window(s32[32,16,128]{2,1,0:T(8,128)S(1)} %fusion.41, s32[]{:T(128)} %constant.65.clone.1), window={size=1x1x128 pad=0_0x0_0x127_0}, to_apply=%region_0.0 | reduce-window | flops 8323072 | bytes 524292 | tf_op jit(solution)/shard_map/reduce-window
  14.8 8.1 %scatter_custom_fusion = f32[4096]{0:T(1024)S(1)} fusion(s32[2048]{0:T(1024)S(1)} %bitcast.84, f32[2048]{0:T(1024)S(1)} %bitcast.88, f32[]{:T(128)} %constant.70.clone.1), kind=kCustom, calls=%fused_computation.160 | custom fusion | bytes 16388 | tf_op jit(solution)/shard_map/scatter | solution.py:71
  22.9 8.1 %scatter_custom_fusion.1 = f32[4096]{0:T(1024)S(1)} fusion(s32[2048]{0:T(1024)S(1)} %bitcast.85, f32[2048]{0:T(1024)S(1)} %bitcast.89, f32[]{:T(128)} %constant.73.clone.1), kind=kCustom, calls=%fused_computation.158 | custom fusion | bytes 16388 | tf_op jit(solution)/shard_map/scatter | solution.py:75
  31.6 8.2 %all-to-all-start = ((f32[2,32,128]{2,0,1:T(2,128)}), f32[2,32,128]{2,0,1:T(2,128)S(1)}, u32[]{:S(2)}, u32[]{:S(2)}) async-start(f32[2,32,128]{2,0,1:T(2,128)} %pad_maximum_fusion.88), calls=%async_computation | async-start | bytes 65536 | tf_op jit(solution)/shard_map/all_to_all | solution.py:77
  39.8 5.9 %copy_add_fusion = (f32[64,32,256]{2,0,1:T(8,128)}, f32[64,32,256]{2,0,1:T(8,128)S(1)}) fusion(f32[64,32,256]{2,1,0:T(8,128)} %param.11, f32[64,32,256]{2,1,0:T(8,128)} %param.10), kind=kLoop, calls=%fused_computation.124 | loop fusion | flops 524288 | bytes 8388608 | tf_op jit(solution)/shard_map/add | solution.py:89
  45.8 1.9 collective-permute-start.12
  47.7 6.0 %collective-permute-start.13 = (f32[1,32,256]{2,0,1:T(1,128)S(1)}, f32[1,32,256]{2,0,1:T(1,128)S(1)}, u32[]{:S(2)}, u32[]{:S(2)}) collective-permute-start(f32[1,32,256]{2,0,1:T(1,128)S(1)} %copy.116), channel_id=1, source_target_pairs={{0,64},{64,128},{128,192},{1,65},{65,129},{129,193},{2,66},{66,130... | collective-permute-start | bytes 98312 | tf_op jit(solution)/shard_map/ppermute | solution.py:16
  54.1 4.8 %collective-permute-start = (f32[16,128,1]{1,0,2:T(8,128)S(1)}, f32[16,128,1]{1,0,2:T(8,128)S(1)}, u32[]{:S(2)}, u32[]{:S(2)}) collective-permute-start(f32[16,128,1]{1,0,2:T(8,128)S(1)} %copy.133), channel_id=1, source_target_pairs={{0,64},{64,128},{128,192},{1,65},{65,129},{129,193},{2,66},{66,130... | collective-permute-start | bytes 24584 | tf_op jit(solution)/shard_map/ppermute | solution.py:16
  59.6 1.9 copy.111
  61.5 2.9 copy.80
  65.1 2.9 collective-permute-start.2
  68.0 6.1 %collective-permute-start.3 = (f32[1,128,258]{1,2,0:T(8,128)}, f32[1,128,258]{1,2,0:T(8,128)}, u32[]{:S(2)}, u32[]{:S(2)}) collective-permute-start(f32[1,128,258]{1,2,0:T(8,128)} %get-tuple-element.40), channel_id=1, source_target_pairs={{0,2},{2,4},{4,6},{6,8},{8,10},{10,12},{12,14},{14,16},{16,18},{18... | collective-permute-start | bytes 396296 | tf_op jit(solution)/shard_map/ppermute | solution.py:16
  74.1 1.9 collective-permute-start.14
  76.1 6.9 %collective-permute-start.15 = (f32[66,1,256]{2,0,1:T(8,128)S(1)}, f32[66,1,256]{2,0,1:T(8,128)S(1)}, u32[]{:S(2)}, u32[]{:S(2)}) collective-permute-start(f32[66,1,256]{2,0,1:T(8,128)S(1)} %get-tuple-element.36), channel_id=1, source_target_pairs={{0,2},{2,4},{4,6},{6,8},{8,10},{10,12},{12,14},{14,16},{16,18},{18... | collective-permute-start | bytes 202760 | tf_op jit(solution)/shard_map/ppermute | solution.py:16
  83.1 23.0 %gather_fusion = f32[4096]{0:T(1024)S(1)} fusion(f32[8192]{0:T(1024)S(1)} %bitcast.54, s32[4096]{0:T(1024)S(1)} %broadcast_clamp_fusion), kind=kCustom, calls=%fused_computation | custom fusion | bytes 49152 | tf_op jit(solution)/shard_map/gather | solution.py:84
  106.8 8.0 %all-to-all-start.1 = ((f32[32,128,1]{1,2,0:T(1,128)}), f32[32,128,1]{1,2,0:T(1,128)S(1)}, u32[]{:S(2)}, u32[]{:S(2)}) async-start(f32[32,128,1]{1,2,0:T(1,128)} %bitcast.19), calls=%async_computation.1 | async-start | bytes 32768 | tf_op jit(solution)/shard_map/all_to_all | solution.py:87
  114.8 29.4 %scatter_custom_fusion.2 = f32[8192]{0:T(1024)} fusion(s32[4096]{0:T(1024)S(1)} %bitcast.87, f32[4096]{0:T(1024)S(1)} %get-tuple-element.20, f32[]{:T(128)} %constant.70.clone.1), kind=kCustom, calls=%fused_computation.153 | custom fusion | flops 4096 | bytes 32772 | tf_op jit(solution)/shard_map/scatter-add | solution.py:86
  145.4 1.8 pad_maximum_fusion
  147.3 1.4 fusion.49
  148.7 2.4 copy.119
  151.1 1.3 collective-permute-start.16
  153.6 4.2 %collective-permute-start.17 = (f32[66,34,1]{0,1,2:T(8,128)}, f32[66,34,1]{0,1,2:T(8,128)}, u32[]{:S(2)}, u32[]{:S(2)}) collective-permute-start(f32[66,34,1]{0,1,2:T(8,128)} %copy.121), channel_id=1, source_target_pairs={{0,1},{2,3},{4,5},{6,7},{8,9},{10,11},{12,13},{14,15},{16,17},{18,... | collective-permute-start | bytes 26936 | tf_op jit(solution)/shard_map/ppermute | solution.py:16
  158.8 1.8 scatter-add.13
  160.6 11.9 %gather_fusion.1 = f32[2048]{0:T(1024)S(1)} fusion(f32[4096]{0:T(1024)S(1)} %bitcast.55, s32[2048]{0:T(1024)} %broadcast_clamp_fusion.1), kind=kCustom, calls=%fused_computation.1 | custom fusion | bytes 24576 | tf_op jit(solution)/shard_map/gather | solution.py:88
  172.5 1.3 copy.120
  173.8 2.3 copy.122
  176.0 13.9 %fusion.23 = f32[64,32,256]{2,0,1:T(8,128)} fusion(f32[64,32,256]{2,0,1:T(8,128)} %copy-done.1, f32[64,32,256]{2,0,1:T(8,128)} %scatter-add.13, f32[66,34,1]{2,0,1:T(8,128)} %copy.122, f32[66,1,256]{2,0,1:T(8,128)} %copy-done.7, f32[66,1,256]{2,0,1:T(8,128)} %copy-done.8, f32[1,32,256]{2,0,1:T(1,128)S(1)} %collective-permute-done.12, ...), kind=kLoop, calls=%fused_computation.56 | loop fusion | flops 14680064 | bytes 6510112 | tf_op jit(solution)/shard_map/add | solution.py:102
  191.1 2.9 fusion.51
  194.0 3.0 copy.86
  197.0 1.3 collective-permute-start.4
  198.3 3.0 copy.88
  201.4 3.0 collective-permute-start.5
  205.5 1.9 collective-permute-start.18
  207.4 6.0 %collective-permute-start.19 = (f32[1,32,256]{2,0,1:T(1,128)S(1)}, f32[1,32,256]{2,0,1:T(1,128)S(1)}, u32[]{:S(2)}, u32[]{:S(2)}) collective-permute-start(f32[1,32,256]{2,0,1:T(1,128)S(1)} %get-tuple-element.42), channel_id=1, source_target_pairs={{0,64},{64,128},{128,192},{1,65},{65,129},{129,193},{2,66},{66,130... | collective-permute-start | bytes 98312 | tf_op jit(solution)/shard_map/ppermute | solution.py:16
  213.5 2.3 copy.87
  215.8 2.2 copy.89
  218.0 8.2 %fusion.2 = (f32[16,128,256]{1,2,0:T(8,128)S(1)}, pred[16,128,256]{1,2,0:T(8,128)(4,1)}) fusion(f32[16,128,256]{1,2,0:T(8,128)S(1)} %copy.111, f32[16,128,1]{1,2,0:T(1,128)S(1)} %bitcast.65, f32[16,128,1]{1,2,0:T(1,128)S(1)} %bitcast.62, f32[18,1,258]{1,2,0:T(8,128)} %copy.89, f32[1,128,258]{1,2,0:T(8,128)S(1)} %collective-permute-done.2, ...), kind=kLoop, calls=%fused_computation.16 | loop fusion | flops 23068672 | bytes 7141920 | tf_op jit(solution)/shard_map/jit(_where)/select_n | solution.py:53
  226.2 1.9 collective-permute-start.6
  228.2 4.8 %collective-permute-start.7 = (f32[16,128,1]{1,0,2:T(8,128)S(1)}, f32[16,128,1]{1,0,2:T(8,128)S(1)}, u32[]{:S(2)}, u32[]{:S(2)}) collective-permute-start(f32[16,128,1]{1,0,2:T(8,128)S(1)} %bitcast.90), channel_id=1, source_target_pairs={{64,0},{128,64},{192,128},{65,1},{129,65},{193,129},{66,2},{130,66... | collective-permute-start | bytes 24584 | tf_op jit(solution)/shard_map/ppermute | solution.py:19
  233.1 2.8 collective-permute-start.20
  235.8 6.1 %collective-permute-start.21 = (f32[66,1,256]{2,0,1:T(8,128)S(1)}, f32[66,1,256]{2,0,1:T(8,128)S(1)}, u32[]{:S(2)}, u32[]{:S(2)}) collective-permute-start(f32[66,1,256]{2,0,1:T(8,128)S(1)} %get-tuple-element.34), channel_id=1, source_target_pairs={{0,2},{2,4},{4,6},{6,8},{8,10},{10,12},{12,14},{14,16},{16,18},{18... | collective-permute-start | bytes 202760 | tf_op jit(solution)/shard_map/ppermute | solution.py:16
  242.7 1.9 collective-permute-start.8
  244.6 6.9 %collective-permute-start.9 = (f32[1,128,258]{1,2,0:T(8,128)}, f32[1,128,258]{1,2,0:T(8,128)}, u32[]{:S(2)}, u32[]{:S(2)}) collective-permute-start(f32[1,128,258]{1,2,0:T(8,128)} %get-tuple-element.38), channel_id=1, source_target_pairs={{0,2},{2,4},{4,6},{6,8},{8,10},{10,12},{12,14},{14,16},{16,18},{18... | collective-permute-start | bytes 396296 | tf_op jit(solution)/shard_map/ppermute | solution.py:16
  253.2 1.5 fusion.48
  254.6 1.8 copy.124
  256.4 1.3 collective-permute-start.22
  257.8 1.1 copy.126
  258.9 4.2 %collective-permute-start.23 = (f32[66,34,1]{0,1,2:T(8,128)}, f32[66,34,1]{0,1,2:T(8,128)}, u32[]{:S(2)}, u32[]{:S(2)}) collective-permute-start(f32[66,34,1]{0,1,2:T(8,128)} %copy.126), channel_id=1, source_target_pairs={{0,1},{2,3},{4,5},{6,7},{8,9},{10,11},{12,13},{14,15},{16,17},{18,... | collective-permute-start | bytes 26936 | tf_op jit(solution)/shard_map/ppermute | solution.py:16
  263.1 1.3 copy.125
  264.4 2.4 copy.127
  266.8 1.8 pad_maximum_fusion.3
  268.5 3.0 fusion.50
  271.5 3.7 %copy.105 = f32[18,1,258]{2,0,1:T(8,128)} copy(f32[18,1,258]{1,2,0:T(8,128)} %get-tuple-element.30) | data formatting | bytes 37152 | tf_op jit(solution)/shard_map/slice | solution.py:19
  275.2 1.3 collective-permute-start.10
  276.5 3.7 %copy.107 = f32[18,1,258]{2,0,1:T(8,128)} copy(f32[18,1,258]{1,2,0:T(8,128)} %get-tuple-element.31) | data formatting | bytes 37152 | tf_op jit(solution)/shard_map/slice | solution.py:17
  280.1 4.2 %collective-permute-start.11 = (f32[18,1,258]{2,0,1:T(8,128)}, f32[18,1,258]{2,0,1:T(8,128)}, u32[]{:S(2)}, u32[]{:S(2)}) collective-permute-start(f32[18,1,258]{2,0,1:T(8,128)} %copy.107), channel_id=1, source_target_pairs={{0,1},{2,3},{4,5},{6,7},{8,9},{10,11},{12,13},{14,15},{16,17},{18,... | collective-permute-start | bytes 55736 | tf_op jit(solution)/shard_map/ppermute | solution.py:16
  284.4 14.3 %fusion.14 = f32[64,32,256]{2,0,1:T(8,128)S(1)} fusion(f32[64,32,256]{2,0,1:T(8,128)} %fusion.23, f32[64,32,256]{2,0,1:T(8,128)} %scatter-add.13, f32[66,34,1]{2,0,1:T(8,128)} %copy.127, f32[66,1,256]{2,0,1:T(8,128)} %copy-done.9, f32[66,1,256]{2,0,1:T(8,128)} %copy-done.10, f32[1,32,256]{2,0,1:T(1,128)S(1)} %collective-permute-done.18, ...), kind=kLoop, calls=%fused_computation.29 | loop fusion | flops 16252928 | bytes 8607264 | tf_op jit(solution)/shard_map/add | solution.py:110
  298.7 2.5 copy.131
  301.3 3.0 copy.106
  304.3 3.1 copy.108
  307.4 11.5 %fusion.5 = f32[16,128,256]{1,2,0:T(8,128)} fusion(f32[16,128,256]{1,2,0:T(8,128)} %copy-done.3, f32[16,128,256]{1,2,0:T(8,128)S(1)} %copy.111, f32[16,128,1]{1,2,0:T(1,128)S(1)} %bitcast.68, f32[16,128,1]{1,2,0:T(1,128)S(1)} %bitcast.71, f32[18,1,258]{1,2,0:T(8,128)} %copy.108, f32[1,128,258]{1,2,0:T(8,128)S(1)} %collective-permute-done.8, ...), kind=kLoop, calls=%fused_computation.19 | loop fusion | flops 22544384 | bytes 7141920 | tf_op jit(solution)/shard_map/jit(_where)/select_n | solution.py:53
  318.9 2.9 copy.130
  (93 shorter events, 12.3 us)
Async XLA Ops:
  0.6 4.2 %copy-start.11 = (s32[1,1,2048,1]{2,3,1,0:T(1,128)S(1)}, s32[1,1,2048,1]{2,3,1,0:T(1,128)}, u32[]{:S(2)}) copy-start(s32[1,1,2048,1]{2,3,1,0:T(1,128)} %param.12) | copy-start | bytes 24580
  2.5 12.2 %copy-start.14 = (s32[1,1,2048]{2,1,0:T(1,128)S(1)}, s32[1,1,2048]{2,1,0:T(1,128)}, u32[]{:S(2)}) copy-start(s32[1,1,2048]{2,1,0:T(1,128)} %param.13) | copy-start | bytes 24580
  2.9 61.5 %collective-permute-start.1 = (f32[16,128,1]{1,0,2:T(8,128)S(1)}, f32[16,128,1]{1,0,2:T(8,128)S(1)}, u32[]{:S(2)}, u32[]{:S(2)}) collective-permute-start(f32[16,128,1]{1,0,2:T(8,128)S(1)} %copy.134), channel_id=1, source_target_pairs={{64,0},{128,64},{192,128},{65,1},{129,65},{193,129},{66,2},{130,66... | collective-permute-start | bytes 24584 | tf_op jit(solution)/shard_map/ppermute | solution.py:19
  31.6 51.4 %all-to-all-start = ((f32[2,32,128]{2,0,1:T(2,128)}), f32[2,32,128]{2,0,1:T(2,128)S(1)}, u32[]{:S(2)}, u32[]{:S(2)}) async-start(f32[2,32,128]{2,0,1:T(2,128)} %pad_maximum_fusion.88), calls=%async_computation | async-start | bytes 65536 | tf_op jit(solution)/shard_map/all_to_all | solution.py:77
  39.8 7.9 %slice-start = ((f32[64,32,256]{2,1,0:T(8,128)}), f32[1,32,256]{2,1,0:T(8,128)S(1)}, s32[]{:S(2)}) async-start(f32[64,32,256]{2,1,0:T(8,128)} %param.10), calls=%async_computation.2 | async-start | bytes 65536 | tf_op jit(solution)/shard_map/slice | solution.py:17
  45.7 13.8 %copy-start.1 = (f32[64,32,256]{2,0,1:T(8,128)}, f32[64,32,256]{2,0,1:T(8,128)S(1)}, u32[]{:S(2)}) copy-start(f32[64,32,256]{2,0,1:T(8,128)S(1)} %get-tuple-element.45) | copy-start | bytes 6291460
  45.8 28.3 %collective-permute-start.12 = (f32[1,32,256]{2,0,1:T(1,128)S(1)}, f32[1,32,256]{2,0,1:T(1,128)S(1)}, u32[]{:S(2)}, u32[]{:S(2)}) collective-permute-start(f32[1,32,256]{2,0,1:T(1,128)S(1)} %slice.268), channel_id=1, source_target_pairs={{64,0},{128,64},{192,128},{65,1},{129,65},{193,129},{66,2},{130,66... | collective-permute-start | bytes 98312 | tf_op jit(solution)/shard_map/ppermute | solution.py:19
  47.7 26.3 %collective-permute-start.13 = (f32[1,32,256]{2,0,1:T(1,128)S(1)}, f32[1,32,256]{2,0,1:T(1,128)S(1)}, u32[]{:S(2)}, u32[]{:S(2)}) collective-permute-start(f32[1,32,256]{2,0,1:T(1,128)S(1)} %copy.116), channel_id=1, source_target_pairs={{0,64},{64,128},{128,192},{1,65},{65,129},{129,193},{2,66},{66,130... | collective-permute-start | bytes 98312 | tf_op jit(solution)/shard_map/ppermute | solution.py:16
  54.1 10.3 %collective-permute-start = (f32[16,128,1]{1,0,2:T(8,128)S(1)}, f32[16,128,1]{1,0,2:T(8,128)S(1)}, u32[]{:S(2)}, u32[]{:S(2)}) collective-permute-start(f32[16,128,1]{1,0,2:T(8,128)S(1)} %copy.133), channel_id=1, source_target_pairs={{0,64},{64,128},{128,192},{1,65},{65,129},{129,193},{2,66},{66,130... | collective-permute-start | bytes 24584 | tf_op jit(solution)/shard_map/ppermute | solution.py:16
  59.5 158.4 %copy-start.15 = (pred[256]{0:T(512)(128)(4,1)}, pred[256]{0:T(512)(128)(4,1)S(1)}, u32[]{:S(2)}) copy-start(pred[256]{0:T(512)(128)(4,1)S(1)} %compare_and_fusion.1) | copy-start | bytes 772
  64.4 9.7 %copy-start.2 = (f32[64,32,256]{2,0,1:T(8,128)S(1)}, f32[64,32,256]{2,0,1:T(8,128)}, u32[]{:S(2)}) copy-start(f32[64,32,256]{2,0,1:T(8,128)} %copy-done.1) | copy-start | bytes 6291460
  65.1 124.9 %collective-permute-start.2 = (f32[1,128,258]{1,2,0:T(8,128)}, f32[1,128,258]{1,2,0:T(8,128)S(1)}, u32[]{:S(2)}, u32[]{:S(2)}) collective-permute-start(f32[1,128,258]{1,2,0:T(8,128)} %get-tuple-element.41), channel_id=1, source_target_pairs={{2,0},{4,2},{6,4},{8,6},{10,8},{12,10},{14,12},{16,14},{18,16},{20... | collective-permute-start | bytes 396296 | tf_op jit(solution)/shard_map/ppermute | solution.py:19
  68.0 122.0 %collective-permute-start.3 = (f32[1,128,258]{1,2,0:T(8,128)}, f32[1,128,258]{1,2,0:T(8,128)}, u32[]{:S(2)}, u32[]{:S(2)}) collective-permute-start(f32[1,128,258]{1,2,0:T(8,128)} %get-tuple-element.40), channel_id=1, source_target_pairs={{0,2},{2,4},{4,6},{6,8},{8,10},{10,12},{12,14},{14,16},{16,18},{18... | collective-permute-start | bytes 396296 | tf_op jit(solution)/shard_map/ppermute | solution.py:16
  74.1 70.1 %copy-start.5 = (f32[1,32,256]{2,0,1:T(1,128)}, f32[1,32,256]{2,0,1:T(1,128)S(1)}, u32[]{:S(2)}) copy-start(f32[1,32,256]{2,0,1:T(1,128)S(1)} %collective-permute-done.13) | copy-start | bytes 98308
  74.1 70.1 %collective-permute-start.14 = (f32[66,1,256]{2,0,1:T(8,128)S(1)}, f32[66,1,256]{2,0,1:T(8,128)S(1)}, u32[]{:S(2)}, u32[]{:S(2)}) collective-permute-start(f32[66,1,256]{2,0,1:T(8,128)S(1)} %get-tuple-element.37), channel_id=1, source_target_pairs={{2,0},{4,2},{6,4},{8,6},{10,8},{12,10},{14,12},{16,14},{18,16},{20... | collective-permute-start | bytes 202760 | tf_op jit(solution)/shard_map/ppermute | solution.py:19
  76.1 68.1 %collective-permute-start.15 = (f32[66,1,256]{2,0,1:T(8,128)S(1)}, f32[66,1,256]{2,0,1:T(8,128)S(1)}, u32[]{:S(2)}, u32[]{:S(2)}) collective-permute-start(f32[66,1,256]{2,0,1:T(8,128)S(1)} %get-tuple-element.36), channel_id=1, source_target_pairs={{0,2},{2,4},{4,6},{6,8},{8,10},{10,12},{12,14},{14,16},{16,18},{18... | collective-permute-start | bytes 202760 | tf_op jit(solution)/shard_map/ppermute | solution.py:16
  106.8 53.8 %all-to-all-start.1 = ((f32[32,128,1]{1,2,0:T(1,128)}), f32[32,128,1]{1,2,0:T(1,128)S(1)}, u32[]{:S(2)}, u32[]{:S(2)}) async-start(f32[32,128,1]{1,2,0:T(1,128)} %bitcast.19), calls=%async_computation.1 | async-start | bytes 32768 | tf_op jit(solution)/shard_map/all_to_all | solution.py:87
  144.2 0.6 copy-start.7
  144.8 0.6 copy-start.8
  151.1 21.3 %collective-permute-start.16 = (f32[66,34,1]{0,1,2:T(8,128)}, f32[66,34,1]{0,1,2:T(8,128)}, u32[]{:S(2)}, u32[]{:S(2)}) collective-permute-start(f32[66,34,1]{0,1,2:T(8,128)} %copy.119), channel_id=1, source_target_pairs={{1,0},{3,2},{5,4},{7,6},{9,8},{11,10},{13,12},{15,14},{17,16},{19,... | collective-permute-start | bytes 26936 | tf_op jit(solution)/shard_map/ppermute | solution.py:19
  153.6 20.2 %collective-permute-start.17 = (f32[66,34,1]{0,1,2:T(8,128)}, f32[66,34,1]{0,1,2:T(8,128)}, u32[]{:S(2)}, u32[]{:S(2)}) collective-permute-start(f32[66,34,1]{0,1,2:T(8,128)} %copy.121), channel_id=1, source_target_pairs={{0,1},{2,3},{4,5},{6,7},{8,9},{10,11},{12,13},{14,15},{16,17},{18,... | collective-permute-start | bytes 26936 | tf_op jit(solution)/shard_map/ppermute | solution.py:16
  172.5 45.5 %copy-start.12 = (f32[2048]{0:T(1024)}, f32[2048]{0:T(1024)S(1)}, u32[]{:S(2)}) copy-start(f32[2048]{0:T(1024)S(1)} %gather_fusion.1) | copy-start | bytes 24580
  197.0 16.4 %collective-permute-start.4 = (f32[18,1,258]{2,0,1:T(8,128)S(1)}, f32[18,1,258]{2,0,1:T(8,128)S(1)}, u32[]{:S(2)}, u32[]{:S(2)}) collective-permute-start(f32[18,1,258]{2,0,1:T(8,128)S(1)} %copy.86), channel_id=1, source_target_pairs={{1,0},{3,2},{5,4},{7,6},{9,8},{11,10},{13,12},{15,14},{17,16},{19,... | collective-permute-start | bytes 55736 | tf_op jit(solution)/shard_map/ppermute | solution.py:19
  201.4 14.4 %collective-permute-start.5 = (f32[18,1,258]{2,0,1:T(8,128)S(1)}, f32[18,1,258]{2,0,1:T(8,128)S(1)}, u32[]{:S(2)}, u32[]{:S(2)}) collective-permute-start(f32[18,1,258]{2,0,1:T(8,128)S(1)} %copy.88), channel_id=1, source_target_pairs={{0,1},{2,3},{4,5},{6,7},{8,9},{10,11},{12,13},{14,15},{16,17},{18,... | collective-permute-start | bytes 55736 | tf_op jit(solution)/shard_map/ppermute | solution.py:16
  205.5 27.5 %collective-permute-start.18 = (f32[1,32,256]{2,0,1:T(1,128)S(1)}, f32[1,32,256]{2,0,1:T(1,128)S(1)}, u32[]{:S(2)}, u32[]{:S(2)}) collective-permute-start(f32[1,32,256]{2,0,1:T(1,128)S(1)} %get-tuple-element.43), channel_id=1, source_target_pairs={{64,0},{128,64},{192,128},{65,1},{129,65},{193,129},{66,2},{130,66... | collective-permute-start | bytes 98312 | tf_op jit(solution)/shard_map/ppermute | solution.py:19
  207.4 25.6 %collective-permute-start.19 = (f32[1,32,256]{2,0,1:T(1,128)S(1)}, f32[1,32,256]{2,0,1:T(1,128)S(1)}, u32[]{:S(2)}, u32[]{:S(2)}) collective-permute-start(f32[1,32,256]{2,0,1:T(1,128)S(1)} %get-tuple-element.42), channel_id=1, source_target_pairs={{0,64},{64,128},{128,192},{1,65},{65,129},{129,193},{2,66},{66,130... | collective-permute-start | bytes 98312 | tf_op jit(solution)/shard_map/ppermute | solution.py:16
  218.0 15.0 %copy-start = (f32[64,32,256]{2,0,1:T(8,128)S(1)}, f32[64,32,256]{2,0,1:T(8,128)}, u32[]{:S(2)}) copy-start(f32[64,32,256]{2,0,1:T(8,128)} %fusion.23) | copy-start | bytes 6291460
  226.2 16.5 %copy-start.3 = (f32[16,128,256]{1,2,0:T(8,128)}, f32[16,128,256]{1,2,0:T(8,128)S(1)}, u32[]{:S(2)}) copy-start(f32[16,128,256]{1,2,0:T(8,128)S(1)} %get-tuple-element.22) | copy-start | bytes 6291460
  226.2 15.7 %collective-permute-start.6 = (f32[16,128,1]{1,0,2:T(8,128)S(1)}, f32[16,128,1]{1,0,2:T(8,128)S(1)}, u32[]{:S(2)}, u32[]{:S(2)}) collective-permute-start(f32[16,128,1]{1,0,2:T(8,128)S(1)} %bitcast.91), channel_id=1, source_target_pairs={{0,64},{64,128},{128,192},{1,65},{65,129},{129,193},{2,66},{66,130... | collective-permute-start | bytes 24584 | tf_op jit(solution)/shard_map/ppermute | solution.py:16
  228.2 13.8 %collective-permute-start.7 = (f32[16,128,1]{1,0,2:T(8,128)S(1)}, f32[16,128,1]{1,0,2:T(8,128)S(1)}, u32[]{:S(2)}, u32[]{:S(2)}) collective-permute-start(f32[16,128,1]{1,0,2:T(8,128)S(1)} %bitcast.90), channel_id=1, source_target_pairs={{64,0},{128,64},{192,128},{65,1},{129,65},{193,129},{66,2},{130,66... | collective-permute-start | bytes 24584 | tf_op jit(solution)/shard_map/ppermute | solution.py:19
  233.0 18.6 %copy-start.6 = (f32[1,32,256]{2,0,1:T(1,128)}, f32[1,32,256]{2,0,1:T(1,128)S(1)}, u32[]{:S(2)}) copy-start(f32[1,32,256]{2,0,1:T(1,128)S(1)} %collective-permute-done.19) | copy-start | bytes 98308
  233.1 18.5 %collective-permute-start.20 = (f32[66,1,256]{2,0,1:T(8,128)S(1)}, f32[66,1,256]{2,0,1:T(8,128)S(1)}, u32[]{:S(2)}, u32[]{:S(2)}) collective-permute-start(f32[66,1,256]{2,0,1:T(8,128)S(1)} %get-tuple-element.35), channel_id=1, source_target_pairs={{2,0},{4,2},{6,4},{8,6},{10,8},{12,10},{14,12},{16,14},{18,16},{20... | collective-permute-start | bytes 202760 | tf_op jit(solution)/shard_map/ppermute | solution.py:19
  235.8 15.8 %collective-permute-start.21 = (f32[66,1,256]{2,0,1:T(8,128)S(1)}, f32[66,1,256]{2,0,1:T(8,128)S(1)}, u32[]{:S(2)}, u32[]{:S(2)}) collective-permute-start(f32[66,1,256]{2,0,1:T(8,128)S(1)} %get-tuple-element.34), channel_id=1, source_target_pairs={{0,2},{2,4},{4,6},{6,8},{8,10},{10,12},{12,14},{14,16},{16,18},{18... | collective-permute-start | bytes 202760 | tf_op jit(solution)/shard_map/ppermute | solution.py:16
  242.7 24.0 %collective-permute-start.8 = (f32[1,128,258]{1,2,0:T(8,128)}, f32[1,128,258]{1,2,0:T(8,128)S(1)}, u32[]{:S(2)}, u32[]{:S(2)}) collective-permute-start(f32[1,128,258]{1,2,0:T(8,128)} %get-tuple-element.39), channel_id=1, source_target_pairs={{2,0},{4,2},{6,4},{8,6},{10,8},{12,10},{14,12},{16,14},{18,16},{20... | collective-permute-start | bytes 396296 | tf_op jit(solution)/shard_map/ppermute | solution.py:19
  244.6 22.1 %collective-permute-start.9 = (f32[1,128,258]{1,2,0:T(8,128)}, f32[1,128,258]{1,2,0:T(8,128)}, u32[]{:S(2)}, u32[]{:S(2)}) collective-permute-start(f32[1,128,258]{1,2,0:T(8,128)} %get-tuple-element.38), channel_id=1, source_target_pairs={{0,2},{2,4},{4,6},{6,8},{8,10},{10,12},{12,14},{14,16},{16,18},{18... | collective-permute-start | bytes 396296 | tf_op jit(solution)/shard_map/ppermute | solution.py:16
  251.6 0.6 copy-start.9
  252.2 0.6 copy-start.10
  256.4 6.7 %collective-permute-start.22 = (f32[66,34,1]{0,1,2:T(8,128)S(1)}, f32[66,34,1]{0,1,2:T(8,128)}, u32[]{:S(2)}, u32[]{:S(2)}) collective-permute-start(f32[66,34,1]{0,1,2:T(8,128)S(1)} %copy.124), channel_id=1, source_target_pairs={{1,0},{3,2},{5,4},{7,6},{9,8},{11,10},{13,12},{15,14},{17,16},{19,... | collective-permute-start | bytes 26936 | tf_op jit(solution)/shard_map/ppermute | solution.py:19
  258.9 5.5 %collective-permute-start.23 = (f32[66,34,1]{0,1,2:T(8,128)}, f32[66,34,1]{0,1,2:T(8,128)}, u32[]{:S(2)}, u32[]{:S(2)}) collective-permute-start(f32[66,34,1]{0,1,2:T(8,128)} %copy.126), channel_id=1, source_target_pairs={{0,1},{2,3},{4,5},{6,7},{8,9},{10,11},{12,13},{14,15},{16,17},{18,... | collective-permute-start | bytes 26936 | tf_op jit(solution)/shard_map/ppermute | solution.py:16
  275.2 26.1 %collective-permute-start.10 = (f32[18,1,258]{2,0,1:T(8,128)}, f32[18,1,258]{2,0,1:T(8,128)}, u32[]{:S(2)}, u32[]{:S(2)}) collective-permute-start(f32[18,1,258]{2,0,1:T(8,128)} %copy.105), channel_id=1, source_target_pairs={{1,0},{3,2},{5,4},{7,6},{9,8},{11,10},{13,12},{15,14},{17,16},{19,... | collective-permute-start | bytes 55736 | tf_op jit(solution)/shard_map/ppermute | solution.py:19
  280.1 24.2 %collective-permute-start.11 = (f32[18,1,258]{2,0,1:T(8,128)}, f32[18,1,258]{2,0,1:T(8,128)}, u32[]{:S(2)}, u32[]{:S(2)}) collective-permute-start(f32[18,1,258]{2,0,1:T(8,128)} %copy.107), channel_id=1, source_target_pairs={{0,1},{2,3},{4,5},{6,7},{8,9},{10,11},{12,13},{14,15},{16,17},{18,... | collective-permute-start | bytes 55736 | tf_op jit(solution)/shard_map/ppermute | solution.py:16
  301.3 6.1 %copy-start.4 = (pred[16,128,256]{1,2,0:T(8,128)(4,1)S(1)}, pred[16,128,256]{1,2,0:T(8,128)(4,1)}, u32[]{:S(2)}) copy-start(pred[16,128,256]{1,2,0:T(8,128)(4,1)} %get-tuple-element.23) | copy-start | bytes 1572868
  301.3 6.1 %copy-start.13 = (f32[2048]{0:T(1024)S(1)}, f32[2048]{0:T(1024)}, u32[]{:S(2)}) copy-start(f32[2048]{0:T(1024)} %copy-done.12) | copy-start | bytes 24580
  301.3 6.1 %copy-start.16 = (pred[256]{0:T(512)(128)(4,1)S(1)}, pred[256]{0:T(512)(128)(4,1)}, u32[]{:S(2)}) copy-start(pred[256]{0:T(512)(128)(4,1)} %copy-done.15) | copy-start | bytes 772
where the time goes:
time: 323 us; the launch traced here: 322 us
  local copies, waits for them, and re-layouts  116 us (36%)
  starting transfers between devices  102 us (32%)
  other arithmetic  102 us (32%)
    ppermute x12, starting transfers between devices, padded_2(): lax.ppermute(lax.slice_in_dim(block, block.shape[dim] - width, None, axis...  60.5 us
    scatter-add x1, other arithmetic, local(): jax.ops.segment_sum(heat_flux, safe_targets, num_segments=fin_width * fin...  29.4 us
    ppermute x12, starting transfers between devices, padded_2(): lax.ppermute(lax.slice_in_dim(block, 0, width, axis=dim), axis, backward)  25.2 us
    gather x1, local copies, waits for them, and re-layouts, local(): fin_wall = jnp.where(valid, surface[safe_targets], 0.0)  23 us
    slice x10, local copies, waits for them, and re-layouts, padded_2(): lax.slice_in_dim(block, 0, width, axis=dim)  21.7 us
    select_n x2, other arithmetic, fluid_update(): return jnp.where(update_mask, updated, field)  19.7 us
    add x1, other arithmetic, local(): omega * (first_state + (fin_rhs - second_image) / diag - fin_temp)  14.3 us
    add x1, other arithmetic, local(): first_state = fin_temp + (fin_rhs - fin_image(fin_temp)) / diag  13.9 us
  transfers between devices with their start and end apart: 26, of which 0 were waited for; matrix products, arithmetic and copies ran while one was open for 56% of the time, Pallas kernels for 0%

commit v1 on v0

--- a/solution.py
+++ b/solution.py
@@ -74,8 +74,16 @@
         .at[slot_index]
         .set(targets.astype(jnp.float32))
     )
-    received = lax.all_to_all(
-        jnp.stack([send_temps, send_targets]), "gx", split_axis=1, concat_axis=1, tiled=True
+    received = jnp.concatenate(
+        lax.all_to_all(
+            jnp.stack(
+                jnp.split(jnp.stack([send_temps, send_targets]), lax.axis_size("gx"), axis=1)
+            ),
+            "gx",
+            0,
+            0,
+        ),
+        axis=1,
     )
     got_targets = received[1].astype(jnp.int32)
     valid = (got_targets >= 0) & on_wall

time: 323 us -> 341 us (1.056)
  other arithmetic: 102 us -> 120 us
    unnamed x0 -> x31, other arithmetic: none -> 17.8 us
  transfers between devices with their start and end apart: 26 -> 26, of which waited for: 0 -> 0; matrix products, arithmetic and copies ran while one was open for 56% -> 58% of each run, Pallas kernels for 0% -> 0%
where the time goes in v1:
time: 341 us; the launch traced here: 340 us
  other arithmetic  120 us (35%)
  local copies, waits for them, and re-layouts  116 us (34%)
  starting transfers between devices  102 us (30%)
    ppermute x12, starting transfers between devices, padded_2(): lax.ppermute(lax.slice_in_dim(block, block.shape[dim] - width, None, axis...  60.5 us
    scatter-add x1, other arithmetic, local(): jax.ops.segment_sum(heat_flux, safe_targets, num_segments=fin_width * fin...  29.4 us
    ppermute x12, starting transfers between devices, padded_2(): lax.ppermute(lax.slice_in_dim(block, 0, width, axis=dim), axis, backward)  25.1 us
    gather x1, local copies, waits for them, and re-layouts, local(): fin_wall = jnp.where(valid, surface[safe_targets], 0.0)  23 us
    slice x10, local copies, waits for them, and re-layouts, padded_2(): lax.slice_in_dim(block, 0, width, axis=dim)  21.7 us
    select_n x2, other arithmetic, fluid_update(): return jnp.where(update_mask, updated, field)  19.8 us
    unnamed x31, other arithmetic  17.8 us
    add x1, other arithmetic, local(): omega * (first_state + (fin_rhs - second_image) / diag - fin_temp)  14.5 us
  transfers between devices with their start and end apart: 26, of which 0 were waited for; matrix products, arithmetic and copies ran while one was open for 58% of the time, Pallas kernels for 0%

profile of v1, /device:TPU:120, one launch (start us, length us, event | category | flops | bytes accessed | tf_op | source)
XLA Modules:
  0.0 339.6 jit_solution(6874252307558144011)
XLA Ops:
  0.6 1.9 fusion.88
  2.9 1.9 collective-permute-start.1
  4.9 9.1 %reduce-window.6 = s32[32,16,128]{2,1,0:T(8,128)S(1)} reduce-window(s32[32,16,128]{2,1,0:T(8,128)S(1)} %fusion.41, s32[]{:T(128)} %constant.65.clone.1), window={size=1x1x128 pad=0_0x0_0x127_0}, to_apply=%region_0.0 | reduce-window | flops 8323072 | bytes 524292 | tf_op jit(solution)/shard_map/reduce-window
  14.8 8.1 %scatter_custom_fusion = f32[4096]{0:T(1024)S(1)} fusion(s32[2048]{0:T(1024)S(1)} %bitcast.218, f32[2048]{0:T(1024)S(1)} %bitcast.222, f32[]{:T(128)} %constant.70.clone.1), kind=kCustom, calls=%fused_computation.257 | custom fusion | bytes 16388 | tf_op jit(solution)/shard_map/scatter | solution.py:71
  22.9 8.1 %scatter_custom_fusion.1 = f32[4096]{0:T(1024)S(1)} fusion(s32[2048]{0:T(1024)S(1)} %bitcast.219, f32[2048]{0:T(1024)S(1)} %bitcast.223, f32[]{:T(128)} %constant.73.clone.1), kind=kCustom, calls=%fused_computation.255 | custom fusion | bytes 16388 | tf_op jit(solution)/shard_map/scatter | solution.py:75
  49.4 8.2 %all-to-all-start = ((f32[32,2,128]{2,1,0:T(2,128)}), f32[32,2,128]{2,1,0:T(2,128)S(1)}, u32[]{:S(2)}, u32[]{:S(2)}) async-start(f32[32,2,128]{2,1,0:T(2,128)} %constant_dynamic-update-slice_fusion), calls=%async_computation | async-start | bytes 65536 | tf_op jit(solution)/shard_map/all_to_all | solution.py:78
  57.6 5.9 %copy_add_fusion = (f32[64,32,256]{2,0,1:T(8,128)}, f32[64,32,256]{2,0,1:T(8,128)S(1)}) fusion(f32[64,32,256]{2,1,0:T(8,128)} %param.11, f32[64,32,256]{2,1,0:T(8,128)} %param.10), kind=kLoop, calls=%fused_computation.124 | loop fusion | flops 524288 | bytes 8388608 | tf_op jit(solution)/shard_map/add | solution.py:97
  63.5 1.9 collective-permute-start.12
  65.5 6.0 %collective-permute-start.13 = (f32[1,32,256]{2,0,1:T(1,128)S(1)}, f32[1,32,256]{2,0,1:T(1,128)S(1)}, u32[]{:S(2)}, u32[]{:S(2)}) collective-permute-start(f32[1,32,256]{2,0,1:T(1,128)S(1)} %copy.114), channel_id=1, source_target_pairs={{0,64},{64,128},{128,192},{1,65},{65,129},{129,193},{2,66},{66,130... | collective-permute-start | bytes 98312 | tf_op jit(solution)/shard_map/ppermute | solution.py:16
  71.9 4.8 %collective-permute-start = (f32[16,128,1]{1,0,2:T(8,128)S(1)}, f32[16,128,1]{1,0,2:T(8,128)S(1)}, u32[]{:S(2)}, u32[]{:S(2)}) collective-permute-start(f32[16,128,1]{1,0,2:T(8,128)S(1)} %copy.131), channel_id=1, source_target_pairs={{0,64},{64,128},{128,192},{1,65},{65,129},{129,193},{2,66},{66,130... | collective-permute-start | bytes 24584 | tf_op jit(solution)/shard_map/ppermute | solution.py:16
  77.3 1.9 copy.109
  79.2 2.9 copy.78
  82.8 2.8 collective-permute-start.2
  85.6 6.1 %collective-permute-start.3 = (f32[1,128,258]{1,2,0:T(8,128)}, f32[1,128,258]{1,2,0:T(8,128)}, u32[]{:S(2)}, u32[]{:S(2)}) collective-permute-start(f32[1,128,258]{1,2,0:T(8,128)} %get-tuple-element.38), channel_id=1, source_target_pairs={{0,2},{2,4},{4,6},{6,8},{8,10},{10,12},{12,14},{14,16},{16,18},{18... | collective-permute-start | bytes 396296 | tf_op jit(solution)/shard_map/ppermute | solution.py:16
  91.8 1.9 collective-permute-start.14
  93.7 6.9 %collective-permute-start.15 = (f32[66,1,256]{2,0,1:T(8,128)S(1)}, f32[66,1,256]{2,0,1:T(8,128)S(1)}, u32[]{:S(2)}, u32[]{:S(2)}) collective-permute-start(f32[66,1,256]{2,0,1:T(8,128)S(1)} %get-tuple-element.34), channel_id=1, source_target_pairs={{0,2},{2,4},{4,6},{6,8},{8,10},{10,12},{12,14},{14,16},{16,18},{18... | collective-permute-start | bytes 202760 | tf_op jit(solution)/shard_map/ppermute | solution.py:16
  100.7 23.0 %gather_fusion = f32[4096]{0:T(1024)S(1)} fusion(f32[8192]{0:T(1024)S(1)} %bitcast.127, s32[4096]{0:T(1024)S(1)} %broadcast_clamp_fusion), kind=kCustom, calls=%fused_computation | custom fusion | bytes 49152 | tf_op jit(solution)/shard_map/gather | solution.py:92
  124.4 8.0 %all-to-all-start.1 = ((f32[32,128,1]{1,2,0:T(1,128)}), f32[32,128,1]{1,2,0:T(1,128)S(1)}, u32[]{:S(2)}, u32[]{:S(2)}) async-start(f32[32,128,1]{1,2,0:T(1,128)} %bitcast.52), calls=%async_computation.1 | async-start | bytes 32768 | tf_op jit(solution)/shard_map/all_to_all | solution.py:95
  132.4 29.4 %scatter_custom_fusion.2 = f32[8192]{0:T(1024)} fusion(s32[4096]{0:T(1024)S(1)} %bitcast.221, f32[4096]{0:T(1024)S(1)} %get-tuple-element.18, f32[]{:T(128)} %constant.70.clone.1), kind=kCustom, calls=%fused_computation.250 | custom fusion | flops 4096 | bytes 32772 | tf_op jit(solution)/shard_map/scatter-add | solution.py:94
  163.0 1.8 pad_maximum_fusion
  164.9 1.4 fusion.83
  166.3 2.4 copy.117
  168.7 1.3 collective-permute-start.16
  170.0 1.1 copy.119
  171.1 4.2 %collective-permute-start.17 = (f32[66,34,1]{0,1,2:T(8,128)}, f32[66,34,1]{0,1,2:T(8,128)}, u32[]{:S(2)}, u32[]{:S(2)}) collective-permute-start(f32[66,34,1]{0,1,2:T(8,128)} %copy.119), channel_id=1, source_target_pairs={{0,1},{2,3},{4,5},{6,7},{8,9},{10,11},{12,13},{14,15},{16,17},{18,... | collective-permute-start | bytes 26936 | tf_op jit(solution)/shard_map/ppermute | solution.py:16
  176.4 1.8 scatter-add.13
  178.1 11.9 %gather_fusion.1 = f32[2048]{0:T(1024)S(1)} fusion(f32[4096]{0:T(1024)S(1)} %bitcast.128, s32[2048]{0:T(1024)} %broadcast_clamp_fusion.1), kind=kCustom, calls=%fused_computation.1 | custom fusion | bytes 24576 | tf_op jit(solution)/shard_map/gather | solution.py:96
  190.1 1.3 copy.118
  191.3 2.3 copy.120
  193.6 13.9 %fusion.23 = f32[64,32,256]{2,0,1:T(8,128)} fusion(f32[64,32,256]{2,0,1:T(8,128)} %copy-done.1, f32[64,32,256]{2,0,1:T(8,128)} %scatter-add.13, f32[66,34,1]{2,0,1:T(8,128)} %copy.120, f32[66,1,256]{2,0,1:T(8,128)} %copy-done.7, f32[66,1,256]{2,0,1:T(8,128)} %copy-done.8, f32[1,32,256]{2,0,1:T(1,128)S(1)} %collective-permute-done.12, ...), kind=kLoop, calls=%fused_computation.56 | loop fusion | flops 14680064 | bytes 6510112 | tf_op jit(solution)/shard_map/add | solution.py:110
  208.6 2.9 fusion.85
  211.6 3.0 copy.84
  214.6 1.3 collective-permute-start.4
  215.9 3.0 copy.86
  218.9 3.0 collective-permute-start.5
  223.1 1.9 collective-permute-start.18
  225.0 6.0 %collective-permute-start.19 = (f32[1,32,256]{2,0,1:T(1,128)S(1)}, f32[1,32,256]{2,0,1:T(1,128)S(1)}, u32[]{:S(2)}, u32[]{:S(2)}) collective-permute-start(f32[1,32,256]{2,0,1:T(1,128)S(1)} %get-tuple-element.40), channel_id=1, source_target_pairs={{0,64},{64,128},{128,192},{1,65},{65,129},{129,193},{2,66},{66,130... | collective-permute-start | bytes 98312 | tf_op jit(solution)/shard_map/ppermute | solution.py:16
  231.1 2.3 copy.85
  233.4 2.2 copy.87
  235.6 8.2 %fusion.2 = (f32[16,128,256]{1,2,0:T(8,128)S(1)}, pred[16,128,256]{1,2,0:T(8,128)(4,1)}) fusion(f32[16,128,256]{1,2,0:T(8,128)S(1)} %copy.109, f32[16,128,1]{1,2,0:T(1,128)S(1)} %bitcast.202, f32[16,128,1]{1,2,0:T(1,128)S(1)} %bitcast.199, f32[18,1,258]{1,2,0:T(8,128)} %copy.87, f32[1,128,258]{1,2,0:T(8,128)S(1)} %collective-permute-done.2, ...), kind=kLoop, calls=%fused_computation.16 | loop fusion | flops 23068672 | bytes 7141920 | tf_op jit(solution)/shard_map/jit(_where)/select_n | solution.py:53
  243.8 1.9 collective-permute-start.6
  245.8 4.8 %collective-permute-start.7 = (f32[16,128,1]{1,0,2:T(8,128)S(1)}, f32[16,128,1]{1,0,2:T(8,128)S(1)}, u32[]{:S(2)}, u32[]{:S(2)}) collective-permute-start(f32[16,128,1]{1,0,2:T(8,128)S(1)} %bitcast.224), channel_id=1, source_target_pairs={{64,0},{128,64},{192,128},{65,1},{129,65},{193,129},{66,2},{130,66... | collective-permute-start | bytes 24584 | tf_op jit(solution)/shard_map/ppermute | solution.py:19
  250.7 2.8 collective-permute-start.20
  253.4 6.1 %collective-permute-start.21 = (f32[66,1,256]{2,0,1:T(8,128)S(1)}, f32[66,1,256]{2,0,1:T(8,128)S(1)}, u32[]{:S(2)}, u32[]{:S(2)}) collective-permute-start(f32[66,1,256]{2,0,1:T(8,128)S(1)} %get-tuple-element.32), channel_id=1, source_target_pairs={{0,2},{2,4},{4,6},{6,8},{8,10},{10,12},{12,14},{14,16},{16,18},{18... | collective-permute-start | bytes 202760 | tf_op jit(solution)/shard_map/ppermute | solution.py:16
  260.3 1.9 collective-permute-start.8
  262.2 6.9 %collective-permute-start.9 = (f32[1,128,258]{1,2,0:T(8,128)}, f32[1,128,258]{1,2,0:T(8,128)}, u32[]{:S(2)}, u32[]{:S(2)}) collective-permute-start(f32[1,128,258]{1,2,0:T(8,128)} %get-tuple-element.36), channel_id=1, source_target_pairs={{0,2},{2,4},{4,6},{6,8},{8,10},{10,12},{12,14},{14,16},{16,18},{18... | collective-permute-start | bytes 396296 | tf_op jit(solution)/shard_map/ppermute | solution.py:16
  270.8 1.5 fusion.82
  272.2 1.8 copy.122
  274.0 1.3 collective-permute-start.22
  276.5 4.2 %collective-permute-start.23 = (f32[66,34,1]{0,1,2:T(8,128)}, f32[66,34,1]{0,1,2:T(8,128)}, u32[]{:S(2)}, u32[]{:S(2)}) collective-permute-start(f32[66,34,1]{0,1,2:T(8,128)} %copy.124), channel_id=1, source_target_pairs={{0,1},{2,3},{4,5},{6,7},{8,9},{10,11},{12,13},{14,15},{16,17},{18,... | collective-permute-start | bytes 26936 | tf_op jit(solution)/shard_map/ppermute | solution.py:16
  280.7 1.3 copy.123
  282.0 2.4 copy.125
  284.4 1.8 pad_maximum_fusion.3
  286.1 3.0 fusion.84
  289.1 3.7 %copy.103 = f32[18,1,258]{2,0,1:T(8,128)} copy(f32[18,1,258]{1,2,0:T(8,128)} %get-tuple-element.28) | data formatting | bytes 37152 | tf_op jit(solution)/shard_map/slice | solution.py:19
  292.8 1.3 collective-permute-start.10
  294.1 3.7 %copy.105 = f32[18,1,258]{2,0,1:T(8,128)} copy(f32[18,1,258]{1,2,0:T(8,128)} %get-tuple-element.29) | data formatting | bytes 37152 | tf_op jit(solution)/shard_map/slice | solution.py:17
  297.8 4.2 %collective-permute-start.11 = (f32[18,1,258]{2,0,1:T(8,128)}, f32[18,1,258]{2,0,1:T(8,128)}, u32[]{:S(2)}, u32[]{:S(2)}) collective-permute-start(f32[18,1,258]{2,0,1:T(8,128)} %copy.105), channel_id=1, source_target_pairs={{0,1},{2,3},{4,5},{6,7},{8,9},{10,11},{12,13},{14,15},{16,17},{18,... | collective-permute-start | bytes 55736 | tf_op jit(solution)/shard_map/ppermute | solution.py:16
  302.0 14.5 %fusion.14 = f32[64,32,256]{2,0,1:T(8,128)S(1)} fusion(f32[64,32,256]{2,0,1:T(8,128)} %fusion.23, f32[64,32,256]{2,0,1:T(8,128)} %scatter-add.13, f32[66,34,1]{2,0,1:T(8,128)} %copy.125, f32[66,1,256]{2,0,1:T(8,128)} %copy-done.9, f32[66,1,256]{2,0,1:T(8,128)} %copy-done.10, f32[1,32,256]{2,0,1:T(1,128)S(1)} %collective-permute-done.18, ...), kind=kLoop, calls=%fused_computation.29 | loop fusion | flops 16252928 | bytes 8607264 | tf_op jit(solution)/shard_map/add | solution.py:118
  316.5 2.5 copy.129
  319.0 3.0 copy.104
  322.1 3.1 copy.106
  325.2 11.5 %fusion.5 = f32[16,128,256]{1,2,0:T(8,128)} fusion(f32[16,128,256]{1,2,0:T(8,128)} %copy-done.3, f32[16,128,256]{1,2,0:T(8,128)S(1)} %copy.109, f32[16,128,1]{1,2,0:T(1,128)S(1)} %bitcast.205, f32[16,128,1]{1,2,0:T(1,128)S(1)} %bitcast.208, f32[18,1,258]{1,2,0:T(8,128)} %copy.106, f32[1,128,258]{1,2,0:T(8,128)S(1)} %collective-permute-done.8, ...), kind=kLoop, calls=%fused_computation.19 | loop fusion | flops 22544384 | bytes 7141920 | tf_op jit(solution)/shard_map/jit(_where)/select_n | solution.py:53
  336.7 2.9 copy.128
  (124 shorter events, 30.0 us)
Async XLA Ops:
  0.6 4.2 %copy-start.11 = (s32[1,1,2048,1]{2,3,1,0:T(1,128)S(1)}, s32[1,1,2048,1]{2,3,1,0:T(1,128)}, u32[]{:S(2)}) copy-start(s32[1,1,2048,1]{2,3,1,0:T(1,128)} %param.12) | copy-start | bytes 24580
  2.5 12.2 %copy-start.14 = (s32[1,1,2048]{2,1,0:T(1,128)S(1)}, s32[1,1,2048]{2,1,0:T(1,128)}, u32[]{:S(2)}) copy-start(s32[1,1,2048]{2,1,0:T(1,128)} %param.13) | copy-start | bytes 24580
  2.9 79.2 %collective-permute-start.1 = (f32[16,128,1]{1,0,2:T(8,128)S(1)}, f32[16,128,1]{1,0,2:T(8,128)S(1)}, u32[]{:S(2)}, u32[]{:S(2)}) collective-permute-start(f32[16,128,1]{1,0,2:T(8,128)S(1)} %copy.132), channel_id=1, source_target_pairs={{64,0},{128,64},{192,128},{65,1},{129,65},{193,129},{66,2},{130,66... | collective-permute-start | bytes 24584 | tf_op jit(solution)/shard_map/ppermute | solution.py:19
  49.4 51.3 %all-to-all-start = ((f32[32,2,128]{2,1,0:T(2,128)}), f32[32,2,128]{2,1,0:T(2,128)S(1)}, u32[]{:S(2)}, u32[]{:S(2)}) async-start(f32[32,2,128]{2,1,0:T(2,128)} %constant_dynamic-update-slice_fusion), calls=%async_computation | async-start | bytes 65536 | tf_op jit(solution)/shard_map/all_to_all | solution.py:78
  57.6 7.9 %slice-start = ((f32[64,32,256]{2,1,0:T(8,128)}), f32[1,32,256]{2,1,0:T(8,128)S(1)}, s32[]{:S(2)}) async-start(f32[64,32,256]{2,1,0:T(8,128)} %param.10), calls=%async_computation.2 | async-start | bytes 65536 | tf_op jit(solution)/shard_map/slice | solution.py:17
  63.5 13.8 %copy-start.1 = (f32[64,32,256]{2,0,1:T(8,128)}, f32[64,32,256]{2,0,1:T(8,128)S(1)}, u32[]{:S(2)}) copy-start(f32[64,32,256]{2,0,1:T(8,128)S(1)} %get-tuple-element.43) | copy-start | bytes 6291460
  63.5 28.2 %collective-permute-start.12 = (f32[1,32,256]{2,0,1:T(1,128)S(1)}, f32[1,32,256]{2,0,1:T(1,128)S(1)}, u32[]{:S(2)}, u32[]{:S(2)}) collective-permute-start(f32[1,32,256]{2,0,1:T(1,128)S(1)} %slice.268), channel_id=1, source_target_pairs={{64,0},{128,64},{192,128},{65,1},{129,65},{193,129},{66,2},{130,66... | collective-permute-start | bytes 98312 | tf_op jit(solution)/shard_map/ppermute | solution.py:19
  65.5 26.2 %collective-permute-start.13 = (f32[1,32,256]{2,0,1:T(1,128)S(1)}, f32[1,32,256]{2,0,1:T(1,128)S(1)}, u32[]{:S(2)}, u32[]{:S(2)}) collective-permute-start(f32[1,32,256]{2,0,1:T(1,128)S(1)} %copy.114), channel_id=1, source_target_pairs={{0,64},{64,128},{128,192},{1,65},{65,129},{129,193},{2,66},{66,130... | collective-permute-start | bytes 98312 | tf_op jit(solution)/shard_map/ppermute | solution.py:16
  71.9 10.3 %collective-permute-start = (f32[16,128,1]{1,0,2:T(8,128)S(1)}, f32[16,128,1]{1,0,2:T(8,128)S(1)}, u32[]{:S(2)}, u32[]{:S(2)}) collective-permute-start(f32[16,128,1]{1,0,2:T(8,128)S(1)} %copy.131), channel_id=1, source_target_pairs={{0,64},{64,128},{128,192},{1,65},{65,129},{129,193},{2,66},{66,130... | collective-permute-start | bytes 24584 | tf_op jit(solution)/shard_map/ppermute | solution.py:16
  77.3 158.3 %copy-start.15 = (pred[256]{0:T(512)(128)(4,1)}, pred[256]{0:T(512)(128)(4,1)S(1)}, u32[]{:S(2)}) copy-start(pred[256]{0:T(512)(128)(4,1)S(1)} %compare_and_fusion.1) | copy-start | bytes 772
  82.1 9.6 %copy-start.2 = (f32[64,32,256]{2,0,1:T(8,128)S(1)}, f32[64,32,256]{2,0,1:T(8,128)}, u32[]{:S(2)}) copy-start(f32[64,32,256]{2,0,1:T(8,128)} %copy-done.1) | copy-start | bytes 6291460
  82.8 124.7 %collective-permute-start.2 = (f32[1,128,258]{1,2,0:T(8,128)}, f32[1,128,258]{1,2,0:T(8,128)S(1)}, u32[]{:S(2)}, u32[]{:S(2)}) collective-permute-start(f32[1,128,258]{1,2,0:T(8,128)} %get-tuple-element.39), channel_id=1, source_target_pairs={{2,0},{4,2},{6,4},{8,6},{10,8},{12,10},{14,12},{16,14},{18,16},{20... | collective-permute-start | bytes 396296 | tf_op jit(solution)/shard_map/ppermute | solution.py:19
  85.6 121.9 %collective-permute-start.3 = (f32[1,128,258]{1,2,0:T(8,128)}, f32[1,128,258]{1,2,0:T(8,128)}, u32[]{:S(2)}, u32[]{:S(2)}) collective-permute-start(f32[1,128,258]{1,2,0:T(8,128)} %get-tuple-element.38), channel_id=1, source_target_pairs={{0,2},{2,4},{4,6},{6,8},{8,10},{10,12},{12,14},{14,16},{16,18},{18... | collective-permute-start | bytes 396296 | tf_op jit(solution)/shard_map/ppermute | solution.py:16
  91.7 70.1 %copy-start.5 = (f32[1,32,256]{2,0,1:T(1,128)}, f32[1,32,256]{2,0,1:T(1,128)S(1)}, u32[]{:S(2)}) copy-start(f32[1,32,256]{2,0,1:T(1,128)S(1)} %collective-permute-done.13) | copy-start | bytes 98308
  91.8 70.0 %collective-permute-start.14 = (f32[66,1,256]{2,0,1:T(8,128)S(1)}, f32[66,1,256]{2,0,1:T(8,128)S(1)}, u32[]{:S(2)}, u32[]{:S(2)}) collective-permute-start(f32[66,1,256]{2,0,1:T(8,128)S(1)} %get-tuple-element.35), channel_id=1, source_target_pairs={{2,0},{4,2},{6,4},{8,6},{10,8},{12,10},{14,12},{16,14},{18,16},{20... | collective-permute-start | bytes 202760 | tf_op jit(solution)/shard_map/ppermute | solution.py:19
  93.7 68.1 %collective-permute-start.15 = (f32[66,1,256]{2,0,1:T(8,128)S(1)}, f32[66,1,256]{2,0,1:T(8,128)S(1)}, u32[]{:S(2)}, u32[]{:S(2)}) collective-permute-start(f32[66,1,256]{2,0,1:T(8,128)S(1)} %get-tuple-element.34), channel_id=1, source_target_pairs={{0,2},{2,4},{4,6},{6,8},{8,10},{10,12},{12,14},{14,16},{16,18},{18... | collective-permute-start | bytes 202760 | tf_op jit(solution)/shard_map/ppermute | solution.py:16
  124.4 53.7 %all-to-all-start.1 = ((f32[32,128,1]{1,2,0:T(1,128)}), f32[32,128,1]{1,2,0:T(1,128)S(1)}, u32[]{:S(2)}, u32[]{:S(2)}) async-start(f32[32,128,1]{1,2,0:T(1,128)} %bitcast.52), calls=%async_computation.1 | async-start | bytes 32768 | tf_op jit(solution)/shard_map/all_to_all | solution.py:95
  161.8 0.6 copy-start.7
  162.4 0.6 copy-start.8
  168.7 21.3 %collective-permute-start.16 = (f32[66,34,1]{0,1,2:T(8,128)}, f32[66,34,1]{0,1,2:T(8,128)}, u32[]{:S(2)}, u32[]{:S(2)}) collective-permute-start(f32[66,34,1]{0,1,2:T(8,128)} %copy.117), channel_id=1, source_target_pairs={{1,0},{3,2},{5,4},{7,6},{9,8},{11,10},{13,12},{15,14},{17,16},{19,... | collective-permute-start | bytes 26936 | tf_op jit(solution)/shard_map/ppermute | solution.py:19
  171.1 20.2 %collective-permute-start.17 = (f32[66,34,1]{0,1,2:T(8,128)}, f32[66,34,1]{0,1,2:T(8,128)}, u32[]{:S(2)}, u32[]{:S(2)}) collective-permute-start(f32[66,34,1]{0,1,2:T(8,128)} %copy.119), channel_id=1, source_target_pairs={{0,1},{2,3},{4,5},{6,7},{8,9},{10,11},{12,13},{14,15},{16,17},{18,... | collective-permute-start | bytes 26936 | tf_op jit(solution)/shard_map/ppermute | solution.py:16
  190.0 45.6 %copy-start.12 = (f32[2048]{0:T(1024)}, f32[2048]{0:T(1024)S(1)}, u32[]{:S(2)}) copy-start(f32[2048]{0:T(1024)S(1)} %gather_fusion.1) | copy-start | bytes 24580
  214.6 16.4 %collective-permute-start.4 = (f32[18,1,258]{2,0,1:T(8,128)S(1)}, f32[18,1,258]{2,0,1:T(8,128)S(1)}, u32[]{:S(2)}, u32[]{:S(2)}) collective-permute-start(f32[18,1,258]{2,0,1:T(8,128)S(1)} %copy.84), channel_id=1, source_target_pairs={{1,0},{3,2},{5,4},{7,6},{9,8},{11,10},{13,12},{15,14},{17,16},{19,... | collective-permute-start | bytes 55736 | tf_op jit(solution)/shard_map/ppermute | solution.py:19
  218.9 14.4 %collective-permute-start.5 = (f32[18,1,258]{2,0,1:T(8,128)S(1)}, f32[18,1,258]{2,0,1:T(8,128)S(1)}, u32[]{:S(2)}, u32[]{:S(2)}) collective-permute-start(f32[18,1,258]{2,0,1:T(8,128)S(1)} %copy.86), channel_id=1, source_target_pairs={{0,1},{2,3},{4,5},{6,7},{8,9},{10,11},{12,13},{14,15},{16,17},{18,... | collective-permute-start | bytes 55736 | tf_op jit(solution)/shard_map/ppermute | solution.py:16
  223.1 27.5 %collective-permute-start.18 = (f32[1,32,256]{2,0,1:T(1,128)S(1)}, f32[1,32,256]{2,0,1:T(1,128)S(1)}, u32[]{:S(2)}, u32[]{:S(2)}) collective-permute-start(f32[1,32,256]{2,0,1:T(1,128)S(1)} %get-tuple-element.41), channel_id=1, source_target_pairs={{64,0},{128,64},{192,128},{65,1},{129,65},{193,129},{66,2},{130,66... | collective-permute-start | bytes 98312 | tf_op jit(solution)/shard_map/ppermute | solution.py:19
  225.0 25.6 %collective-permute-start.19 = (f32[1,32,256]{2,0,1:T(1,128)S(1)}, f32[1,32,256]{2,0,1:T(1,128)S(1)}, u32[]{:S(2)}, u32[]{:S(2)}) collective-permute-start(f32[1,32,256]{2,0,1:T(1,128)S(1)} %get-tuple-element.40), channel_id=1, source_target_pairs={{0,64},{64,128},{128,192},{1,65},{65,129},{129,193},{2,66},{66,130... | collective-permute-start | bytes 98312 | tf_op jit(solution)/shard_map/ppermute | solution.py:16
  235.6 15.0 %copy-start = (f32[64,32,256]{2,0,1:T(8,128)S(1)}, f32[64,32,256]{2,0,1:T(8,128)}, u32[]{:S(2)}) copy-start(f32[64,32,256]{2,0,1:T(8,128)} %fusion.23) | copy-start | bytes 6291460
  243.8 16.5 %copy-start.3 = (f32[16,128,256]{1,2,0:T(8,128)}, f32[16,128,256]{1,2,0:T(8,128)S(1)}, u32[]{:S(2)}) copy-start(f32[16,128,256]{1,2,0:T(8,128)S(1)} %get-tuple-element.20) | copy-start | bytes 6291460
  243.8 15.7 %collective-permute-start.6 = (f32[16,128,1]{1,0,2:T(8,128)S(1)}, f32[16,128,1]{1,0,2:T(8,128)S(1)}, u32[]{:S(2)}, u32[]{:S(2)}) collective-permute-start(f32[16,128,1]{1,0,2:T(8,128)S(1)} %bitcast.225), channel_id=1, source_target_pairs={{0,64},{64,128},{128,192},{1,65},{65,129},{129,193},{2,66},{66,130... | collective-permute-start | bytes 24584 | tf_op jit(solution)/shard_map/ppermute | solution.py:16
  245.8 13.8 %collective-permute-start.7 = (f32[16,128,1]{1,0,2:T(8,128)S(1)}, f32[16,128,1]{1,0,2:T(8,128)S(1)}, u32[]{:S(2)}, u32[]{:S(2)}) collective-permute-start(f32[16,128,1]{1,0,2:T(8,128)S(1)} %bitcast.224), channel_id=1, source_target_pairs={{64,0},{128,64},{192,128},{65,1},{129,65},{193,129},{66,2},{130,66... | collective-permute-start | bytes 24584 | tf_op jit(solution)/shard_map/ppermute | solution.py:19
  250.6 18.6 %copy-start.6 = (f32[1,32,256]{2,0,1:T(1,128)}, f32[1,32,256]{2,0,1:T(1,128)S(1)}, u32[]{:S(2)}) copy-start(f32[1,32,256]{2,0,1:T(1,128)S(1)} %collective-permute-done.19) | copy-start | bytes 98308
  250.7 18.5 %collective-permute-start.20 = (f32[66,1,256]{2,0,1:T(8,128)S(1)}, f32[66,1,256]{2,0,1:T(8,128)S(1)}, u32[]{:S(2)}, u32[]{:S(2)}) collective-permute-start(f32[66,1,256]{2,0,1:T(8,128)S(1)} %get-tuple-element.33), channel_id=1, source_target_pairs={{2,0},{4,2},{6,4},{8,6},{10,8},{12,10},{14,12},{16,14},{18,16},{20... | collective-permute-start | bytes 202760 | tf_op jit(solution)/shard_map/ppermute | solution.py:19
  253.4 15.8 %collective-permute-start.21 = (f32[66,1,256]{2,0,1:T(8,128)S(1)}, f32[66,1,256]{2,0,1:T(8,128)S(1)}, u32[]{:S(2)}, u32[]{:S(2)}) collective-permute-start(f32[66,1,256]{2,0,1:T(8,128)S(1)} %get-tuple-element.32), channel_id=1, source_target_pairs={{0,2},{2,4},{4,6},{6,8},{8,10},{10,12},{12,14},{14,16},{16,18},{18... | collective-permute-start | bytes 202760 | tf_op jit(solution)/shard_map/ppermute | solution.py:16
  260.3 24.0 %collective-permute-start.8 = (f32[1,128,258]{1,2,0:T(8,128)}, f32[1,128,258]{1,2,0:T(8,128)S(1)}, u32[]{:S(2)}, u32[]{:S(2)}) collective-permute-start(f32[1,128,258]{1,2,0:T(8,128)} %get-tuple-element.37), channel_id=1, source_target_pairs={{2,0},{4,2},{6,4},{8,6},{10,8},{12,10},{14,12},{16,14},{18,16},{20... | collective-permute-start | bytes 396296 | tf_op jit(solution)/shard_map/ppermute | solution.py:19
  262.2 22.1 %collective-permute-start.9 = (f32[1,128,258]{1,2,0:T(8,128)}, f32[1,128,258]{1,2,0:T(8,128)}, u32[]{:S(2)}, u32[]{:S(2)}) collective-permute-start(f32[1,128,258]{1,2,0:T(8,128)} %get-tuple-element.36), channel_id=1, source_target_pairs={{0,2},{2,4},{4,6},{6,8},{8,10},{10,12},{12,14},{14,16},{16,18},{18... | collective-permute-start | bytes 396296 | tf_op jit(solution)/shard_map/ppermute | solution.py:16
  269.2 0.6 copy-start.9
  269.8 0.6 copy-start.10
  274.0 6.7 %collective-permute-start.22 = (f32[66,34,1]{0,1,2:T(8,128)S(1)}, f32[66,34,1]{0,1,2:T(8,128)}, u32[]{:S(2)}, u32[]{:S(2)}) collective-permute-start(f32[66,34,1]{0,1,2:T(8,128)S(1)} %copy.122), channel_id=1, source_target_pairs={{1,0},{3,2},{5,4},{7,6},{9,8},{11,10},{13,12},{15,14},{17,16},{19,... | collective-permute-start | bytes 26936 | tf_op jit(solution)/shard_map/ppermute | solution.py:19
  276.5 5.5 %collective-permute-start.23 = (f32[66,34,1]{0,1,2:T(8,128)}, f32[66,34,1]{0,1,2:T(8,128)}, u32[]{:S(2)}, u32[]{:S(2)}) collective-permute-start(f32[66,34,1]{0,1,2:T(8,128)} %copy.124), channel_id=1, source_target_pairs={{0,1},{2,3},{4,5},{6,7},{8,9},{10,11},{12,13},{14,15},{16,17},{18,... | collective-permute-start | bytes 26936 | tf_op jit(solution)/shard_map/ppermute | solution.py:16
  292.8 26.2 %collective-permute-start.10 = (f32[18,1,258]{2,0,1:T(8,128)}, f32[18,1,258]{2,0,1:T(8,128)}, u32[]{:S(2)}, u32[]{:S(2)}) collective-permute-start(f32[18,1,258]{2,0,1:T(8,128)} %copy.103), channel_id=1, source_target_pairs={{1,0},{3,2},{5,4},{7,6},{9,8},{11,10},{13,12},{15,14},{17,16},{19,... | collective-permute-start | bytes 55736 | tf_op jit(solution)/shard_map/ppermute | solution.py:19
  297.8 24.3 %collective-permute-start.11 = (f32[18,1,258]{2,0,1:T(8,128)}, f32[18,1,258]{2,0,1:T(8,128)}, u32[]{:S(2)}, u32[]{:S(2)}) collective-permute-start(f32[18,1,258]{2,0,1:T(8,128)} %copy.105), channel_id=1, source_target_pairs={{0,1},{2,3},{4,5},{6,7},{8,9},{10,11},{12,13},{14,15},{16,17},{18,... | collective-permute-start | bytes 55736 | tf_op jit(solution)/shard_map/ppermute | solution.py:16
  319.0 6.1 %copy-start.4 = (pred[16,128,256]{1,2,0:T(8,128)(4,1)S(1)}, pred[16,128,256]{1,2,0:T(8,128)(4,1)}, u32[]{:S(2)}) copy-start(pred[16,128,256]{1,2,0:T(8,128)(4,1)} %get-tuple-element.21) | copy-start | bytes 1572868
  319.0 6.1 %copy-start.13 = (f32[2048]{0:T(1024)S(1)}, f32[2048]{0:T(1024)}, u32[]{:S(2)}) copy-start(f32[2048]{0:T(1024)} %copy-done.12) | copy-start | bytes 24580
  319.0 6.1 %copy-start.16 = (pred[256]{0:T(512)(128)(4,1)S(1)}, pred[256]{0:T(512)(128)(4,1)}, u32[]{:S(2)}) copy-start(pred[256]{0:T(512)(128)(4,1)} %copy-done.15) | copy-start | bytes 772
